TPU v7x, 1024 devices: a whole 4x4x32 slice. The times are simulated.
1024 devices in a mesh: grp: 8 (over y, core), rep: 128 (over z, x).
Axes of the slice: x: 4, y: 4, z: 32, core: 2. Of those that a mesh axis runs over, the one named last changes fastest.
Arguments:
- queries: bfloat16 [131072, 1024], P(('grp', 'rep')), may hold values from -0.5 to 0.5
- passages: bfloat16 [131072, 1024], P(('grp', 'rep')), may hold values from -0.5 to 0.5
- bank: bfloat16 [512, 1024], P('rep'), may hold values from -0.5 to 0.5
- hard_ids: int32 [131072, 7], P(('grp', 'rep')), may hold values from 0 to 511
- weights: float32 [131072], P(('grp', 'rep')), may hold values from 0.5 to 2
Outputs:
- losses: float32 [131072], P(('grp', 'rep'))
- query_grad: float32 [131072, 1024], P(('grp', 'rep'))
- passage_grad: float32 [131072, 1024], P(('grp', 'rep'))
- bank_grad: float32 [512, 1024], P('rep')
Inputs may be any that keep to these rules, and one draw needn't show every extreme that they name: hard_ids[b, k] is a row of bank, held by index hard_ids[b, k] // 4 of rep; rows may repeat, and a few rows are named far more often than others.
All inputs are finite; a program needn't handle non-finite values.
Results may differ from a plain program's by a relative error of at most 0.0065.
The roundings to bfloat16 on the way count: a program that leaves them out, or rounds other values in their place, can miss the bound.
Values may be sent and summed in bfloat16 or wider, within the bound.
A program may use at most 32 MiB of HBM per device.

v0:
```python
import jax
import jax.numpy as jnp
from jax import lax
from jax.sharding import PartitionSpec as P

logit_divisor_heat = 0.05
epsilon = 1e-06


def unit_rows(values):
    widened = values.astype(jnp.float32)
    inverse = 1.0 / jnp.sqrt(jnp.sum(widened * widened, axis=-1, keepdims=True) + epsilon)
    return (widened * inverse, inverse)


def unit_backward(unit_vec, inverse, upstream):
    return inverse * (upstream - unit_vec * jnp.sum(unit_vec * upstream, axis=-1, keepdims=True))


def contrast(
    search_latent_entries,
    document_cohort_entries,
    distractor_entries,
    sample_importance_list,
    positive,
):
    cohort_logit_table = (
        jnp.dot(
            search_latent_entries, document_cohort_entries.T, preferred_element_type=jnp.float32
        )
        / logit_divisor_heat
    )
    distractor_logit_table = (
        jnp.einsum(
            "ch,clh->cl",
            search_latent_entries,
            distractor_entries,
            preferred_element_type=jnp.float32,
        )
        / logit_divisor_heat
    )
    summed = jnp.sum(jnp.exp(cohort_logit_table), axis=1) + jnp.sum(
        jnp.exp(distractor_logit_table), axis=1
    )
    log_total = jnp.log(summed)
    correct_pair_indicator = (
        jnp.arange(document_cohort_entries.shape[0], dtype=jnp.int32)[None, :] == positive[:, None]
    ).astype(jnp.float32)
    losses = log_total - jnp.sum(correct_pair_indicator * cohort_logit_table, axis=1)
    cohort_likelihood = jnp.exp(cohort_logit_table - log_total[:, None])
    distractor_likelihood = jnp.exp(distractor_logit_table - log_total[:, None])
    cohort_logit_slope = (
        sample_importance_list[:, None]
        * (cohort_likelihood - correct_pair_indicator)
        / logit_divisor_heat
    ).astype(jnp.bfloat16)
    distractor_logit_slope = (
        sample_importance_list[:, None] * distractor_likelihood / logit_divisor_heat
    ).astype(jnp.bfloat16)
    query_up = jnp.dot(
        cohort_logit_slope, document_cohort_entries, preferred_element_type=jnp.float32
    )
    query_up = query_up + jnp.einsum(
        "mk,mkd->md", distractor_logit_slope, distractor_entries, preferred_element_type=jnp.float32
    )
    return (losses, query_up, cohort_logit_slope, distractor_logit_slope)


def bank_terms(row_ids, distractor_logit_slope, search_latent_entries, row_count):
    selector = (
        row_ids[:, :, None] == jnp.arange(row_count, dtype=jnp.int32)[None, None, :]
    ).astype(jnp.bfloat16)
    weighted = (selector * distractor_logit_slope[:, :, None]).reshape(-1, row_count)
    repeated = jnp.broadcast_to(
        search_latent_entries[:, None, :],
        (row_ids.shape[0], row_ids.shape[1], search_latent_entries.shape[1]),
    ).reshape(-1, search_latent_entries.shape[1])
    return jnp.dot(weighted.T, repeated, preferred_element_type=jnp.float32)


def pick_rows(flat_ids, block_rows):
    offsets = jnp.arange(block_rows.shape[0], dtype=jnp.int32)
    selector = (flat_ids[:, None] == offsets[None, :]).astype(jnp.bfloat16)
    return jnp.dot(selector, block_rows, preferred_element_type=jnp.float32)


def body(queries, passages, bank, hard_ids, weights):
    owners_count = lax.axis_size("rep")
    local_rows = queries.shape[0]
    feature_width = queries.shape[1]
    row_count = bank.shape[0] * owners_count
    query_unit, query_inverse = unit_rows(queries)
    passage_unit, passage_inverse = unit_rows(passages)
    bank_unit, bank_inverse = unit_rows(bank)
    search_latent_entries = query_unit.astype(jnp.bfloat16)
    passage_rows = passage_unit.astype(jnp.bfloat16)
    bank_rows = bank_unit.astype(jnp.bfloat16)
    document_cohort_entries = lax.all_gather(passage_rows, "grp", axis=0, tiled=True)
    flat_ids = hard_ids.reshape(-1)
    picked = pick_rows(flat_ids, lax.all_gather(bank_rows, "rep", axis=0, tiled=True))
    distractor_entries = picked.astype(jnp.bfloat16).reshape(
        local_rows, hard_ids.shape[1], feature_width
    )
    positive = lax.axis_index("grp") * local_rows + jnp.arange(local_rows, dtype=jnp.int32)
    losses, query_up, cohort_logit_slope, distractor_logit_slope = contrast(
        search_latent_entries, document_cohort_entries, distractor_entries, weights, positive
    )
    passage_terms = jnp.dot(
        cohort_logit_slope.T, search_latent_entries, preferred_element_type=jnp.float32
    )
    passage_up = lax.psum_scatter(passage_terms, "grp", scatter_dimension=0, tiled=True)
    bank_local = bank_terms(hard_ids, distractor_logit_slope, search_latent_entries, row_count)
    owner_part = lax.psum_scatter(bank_local, "rep", scatter_dimension=0, tiled=True)
    bank_up = lax.psum(owner_part, "grp")
    query_grad = unit_backward(query_unit, query_inverse, query_up)
    passage_grad = unit_backward(passage_unit, passage_inverse, passage_up)
    bank_grad = unit_backward(bank_unit, bank_inverse, bank_up)
    return (losses, query_grad, passage_grad, bank_grad)


def solution(mesh):
    placed = (
        P(("grp", "rep"), None),
        P(("grp", "rep"), None),
        P("rep", None),
        P(("grp", "rep"), None),
        P(("grp", "rep")),
    )
    return jax.shard_map(
        body,
        mesh=mesh,
        in_specs=placed,
        out_specs=(
            P(("grp", "rep")),
            P(("grp", "rep"), None),
            P(("grp", "rep"), None),
            P("rep", None),
        ),
        check_vma=False,
    )
```

profile of v0, /device:TPU:1, one launch (start us, length us, event | category | flops | bytes accessed | tf_op | source)
XLA Modules:
  0.0 893.7 jit_solution(5914982473727241790)
XLA Ops:
  7.2 0.9 fusion.31
  8.1 1.4 fusion.32
  9.5 1.1 fusion.20
  10.6 1.8 fusion.9
  12.5 0.8 copy.10
  13.3 0.2 eq.20
  13.5 1.1 fusion.16
  14.6 1.1 fusion.12
  15.8 235.5 %all-gather.6.cloned.1.call-done = bf16[128,4,1024]{2,1,0:T(4,128)(2,1)} async-done(((bf16[1,4,1024]{2,1,0:T(4,128)(2,1)}), bf16[128,4,1024]{2,1,0:T(4,128)(2,1)}) %all-gather.6.cloned.1.call-update) | async-done | bytes 1048592 | tf_op jit(solution)/shard_map/all_gather | solution.py:100
  251.2 1.3 reshape.54
  252.6 2.4 fusion.2
  255.0 2.6 reshape.52
  257.6 1.2 fusion.21
  259.0 52.2 %all-gather.4.cloned.1.call-done = bf16[1024,1024]{1,0:T(8,128)(2,1)} async-done(((bf16[128,1024]{1,0:T(8,128)(2,1)}), bf16[1024,1024]{1,0:T(8,128)(2,1)}) %all-gather.4.cloned.1.call-update) | async-done | bytes 2097168 | tf_op jit(solution)/shard_map/all_gather | solution.py:98
  311.1 2.6 select_reduce_fusion
  313.7 0.5 fusion.35
  314.3 2.6 convolution_bitcast_fusion
  317.0 2.8 fusion.34
  319.8 1.3 dynamic-slice
  321.8 0.1 copy.13
  321.9 0.7 fusion.36
  322.6 0.9 copy-done.2
  323.5 0.8 fusion.13
  324.3 1.0 fusion.15
  325.3 490.4 %all-reduce.3.cloned.1.call-done = f32[512,1024]{1,0:T(8,128)} async-done(((f32[512,1024]{1,0:T(8,128)}), f32[512,1024]{1,0:T(8,128)}) %all-reduce.3.cloned.1.call-update) | async-done | bytes 2097168
  815.7 0.8 constant_dynamic-slice_fusion
  816.5 40.8 %psum.7 = f32[4,1024]{1,0:T(4,128)S(1)} all-reduce(f32[4,1024]{1,0:T(4,128)S(1)} %constant_dynamic-slice_fusion), channel_id=1, replica_groups=mesh['grp'=8,'rep'=128] {'grp'}, use_global_device_ids=true, to_apply=%region_10.0 | all-reduce | flops 4096 | bytes 32768 | tf_op jit(solution)/shard_map/psum | solution.py:114
  857.3 0.2 fusion.28
  857.5 0.7 fusion.30
  858.2 25.7 %reduce-scatter.2.cloned.1.call-done = f32[128,1024]{1,0:T(8,128)} async-done(((f32[1024,1024]{1,0:T(8,128)}), f32[128,1024]{1,0:T(8,128)}) %reduce-scatter.2.cloned.1.call-update) | async-done | bytes 524304 | tf_op jit(solution)/shard_map/reduce_scatter | solution.py:111
  883.9 1.3 fusion.17
  885.1 2.1 fusion.19
  (28 shorter events, 0.5 us)
Async XLA Ops:
  7.2 8.5 copy-start
  7.2 244.1 %all-gather.6.cloned.1.call-start = ((), (), s32[]{:S(2)}) async-start(), calls=%async_computation.3 | async-start | bytes 1056768 | tf_op jit(solution)/shard_map/all_gather | solution.py:100
  9.5 301.7 %all-gather.4.cloned.1.call-start = ((), (), s32[]{:S(2)}) async-start(), calls=%async_computation.1 | async-start | bytes 2359296 | tf_op jit(solution)/shard_map/all_gather | solution.py:98
  12.4 803.3 %all-reduce.3.cloned.1.call-start = ((), (), s32[]{:S(2)}) async-start(), calls=%async_computation.4 | async-start | bytes 4194304
  258.8 55.4 %copy-start.4 = (f32[128]{0:T(128)S(1)}, f32[128]{0:T(128)}, u32[]{:S(2)}) copy-start(f32[128]{0:T(128)} %param.9) | copy-start | bytes 1540
  258.8 55.4 %copy-start.5 = (s32[128,7]{0,1:T(8,128)S(1)}, s32[128,7]{0,1:T(8,128)}, u32[]{:S(2)}) copy-start(s32[128,7]{0,1:T(8,128)} %param.8) | copy-start | bytes 10756
  316.9 567.0 %reduce-scatter.2.cloned.1.call-start = ((), (), s32[]{:S(2)}) async-start(), calls=%async_computation.2 | async-start | bytes 4718592 | tf_op jit(solution)/shard_map/reduce_scatter | solution.py:111
  321.9 1.6 copy-start.2
  323.5 533.8 %copy-start.3 = (bf16[4,1024]{1,0:T(4,128)(2,1)S(1)}, bf16[4,1024]{1,0:T(4,128)(2,1)}, u32[]{:S(2)}) copy-start(bf16[4,1024]{1,0:T(4,128)(2,1)} %param.7) | copy-start | bytes 24580
  323.5 560.4 %copy-start.1 = (bf16[128,1024]{1,0:T(8,128)(2,1)S(1)}, bf16[128,1024]{1,0:T(8,128)(2,1)}, u32[]{:S(2)}) copy-start(bf16[128,1024]{1,0:T(8,128)(2,1)} %param.6) | copy-start | bytes 786436
Sparse Core Ops, SparseCore 0:
  12.7 238.5 all-gather.5
  254.6 56.5 all-gather.3
  317.1 498.6 all-reduce.2
  819.0 64.8 reduce-scatter.1
where the time goes:
time: 895 us; the launch traced here: 894 us
  waiting for transfers between devices  804 us (90%)
  blocking collectives  40.8 us (5%)
  between operations  14.5 us (2%)
  other arithmetic  13.2 us (1%)
  matrix products  13.1 us (1%)
    unnamed x5, waiting for transfers between devices  490 us
    all_gather x1, waiting for transfers between devices, body(): lax.all_gather(bank_rows, 'rep', axis=0, tiled=True)  235 us
    all_gather x1, waiting for transfers between devices, body(): lax.all_gather(passage_rows, 'grp', axis=0, tiled=True)  52.2 us
    psum x1, blocking collectives, body(): bank_up = lax.psum(owner_part, 'grp')  40.8 us
    reduce_scatter x1, waiting for transfers between devices, body(): lax.psum_scatter(passage_terms, 'grp', scatter_dimension=0, tiled=True)  25.7 us
  transfers between devices with their start and end apart: 4, of which 4 were waited for; matrix products, arithmetic and copies ran while one was open for 2% of the time, Pallas kernels for 0%

commit v1 on v0

v1 whole, which is shorter than its diff:
```python
import functools

import jax
import jax.numpy as jnp
from jax import lax
from jax.experimental import pallas as pl
from jax.experimental.pallas import tpu as pltpu
from jax.sharding import PartitionSpec as P

MESH = pl.DeviceIdType.MESH
F32 = jnp.float32
BF16 = jnp.bfloat16
EPS = 1e-06
HEAT = 20.0
NX = 4
GROUP = 8
ROW_OF = [2 * ((m >> 2 & 1) ^ (m >> 1 & 1)) + (m & 1) for m in range(GROUP)]


def dot_nt(left, right):
    return lax.dot_general(left, right, (((1,), (1,)), ((), ())), preferred_element_type=F32)


def dot_tn(left, right):
    return lax.dot_general(left, right, (((0,), (0,)), ((), ())), preferred_element_type=F32)


def dot_nn(left, right):
    return jnp.dot(left, right, preferred_element_type=F32)


def kernel(
    nz,
    nx,
    q_in,
    p_in,
    bank_in,
    ids_in,
    w_in,
    loss_out,
    qg_out,
    pg_out,
    bg_out,
    q_raw,
    p_raw,
    bank_raw,
    meta_raw,
    w_raw,
    rows_q,
    cols,
    bank_x,
    own_row,
    gathered,
    wide,
    meta,
    sums,
    e_t,
    g_t,
    bank_out,
    plane_in,
    z_out,
    z_in,
    g_in,
    bank_up,
    pu_out,
    pu_in,
    qs_out,
    qs_in,
    qy_out,
    qy_in,
    local_sem,
    send_sem,
    recv_sem,
    zf_send,
    zf_recv,
    zb_send,
    zb_recv,
):
    g, r = lax.axis_index("grp"), lax.axis_index("rep")
    y, c = g // 2, g % 2
    z, x = r // nx, r % nx
    a = y // 2
    b = ((y + 1) // 2) % 2
    share = 2 * b + c
    y_q = y + 1 - 2 * (y % 2)
    y_p = 3 - y
    half = nz // 2
    n = q_raw.shape[0]
    depth = q_raw.shape[1]
    lanes = 128
    groups = depth // lanes
    nb = nx * nz

    def at(z_, x_, y_, c_):
        return (y_ * 2 + c_, z_ * nx + x_)

    def member(m):
        cc = 1 - c if m & 1 else c
        hi = m >> 1
        yy = (y, y_q, None, y_p)[hi] if hi != 2 else 3 - y_q
        return at(z, x, yy, cc)

    loads = [
        pltpu.make_async_copy(src, dst, local_sem.at[i])
        for i, (src, dst) in enumerate(
            [(bank_in, bank_raw), (q_in, q_raw), (p_in, p_raw), (ids_in, meta_raw), (w_in, w_raw)]
        )
    ]
    for load in loads:
        load.start()

    barrier = pltpu.get_barrier_semaphore()

    def greet(device):
        pl.semaphore_signal(barrier, inc=1, device_id=device, device_id_type=MESH)

    def greet_z(i, carry):
        greet(at(lax.rem(z + i, nz), x, y, c))
        return carry

    lax.fori_loop(1, nz, greet_z, 0)
    for dx in range(1, nx):
        for yy in (y, y_p):
            greet(at(z, lax.rem(x + dx, nx), yy, c))
    for m in range(1, GROUP):
        greet(member(m))

    def remote(src, dst, send, recv, device):
        return pltpu.make_async_remote_copy(
            src_ref=src, dst_ref=dst, send_sem=send, recv_sem=recv, device_id=device, device_id_type=MESH
        )

    started = []

    def send(src, dst, index, device):
        copy = remote(src, dst, send_sem.at[index], recv_sem.at[index], device)
        copy.start()
        started.append(copy)
        return copy

    loads[0].wait()
    bank_f = bank_raw[...].astype(F32)
    for j in range(groups):
        bank_x[:, j, :] = bank_f[:, j * lanes : (j + 1) * lanes]
    bank_values = bank_x[...]
    bank_inv = 1.0 / jnp.sqrt(jnp.sum(jnp.sum(bank_values * bank_values, axis=2, keepdims=True), axis=1, keepdims=True) + EPS)
    bank_unit = bank_values * bank_inv
    bank_x[...] = bank_unit
    own_row[...] = bank_x[share].astype(BF16)

    @pl.when(a == 0)
    def _():
        gathered[0, half // 2, 0] = own_row[...]

    loads[1].wait()
    loads[3].wait()
    loads[4].wait()

    def units(raw):
        values = raw[...].astype(F32)
        inv = 1.0 / jnp.sqrt(jnp.sum(values * values, axis=1, keepdims=True) + EPS)
        return values * inv, inv

    q_unit, q_inv = units(q_raw)
    rows_q[0] = q_unit.astype(BF16)
    meta[0, 0:7, :] = meta_raw[...].astype(F32)
    meta[0, 7:8, :] = w_raw[...]
    loads[2].wait()
    p_unit, p_inv = units(p_raw)
    cols[0:n, :] = p_unit.astype(BF16)

    pl.semaphore_wait(barrier, nz - 1 + 2 * (nx - 1) + GROUP - 1)

    def z_forward(k, carry):
        offset = 2 * k + a - half

        @pl.when(offset != 0)
        def _():
            remote(
                own_row,
                gathered.at[0, k, a],
                zf_send.at[k],
                zf_recv.at[k],
                at(lax.rem(z - offset + nz, nz), x, y, c),
            ).start()

        return carry

    lax.fori_loop(0, half, z_forward, 0)

    sibling = member(1)
    neighbour = member(2)
    partner = member(6)
    to_meta = [send(meta.at[0], meta.at[m], m - 1, member(m)) for m in (1, 2, 3)]
    to_q = send(rows_q.at[0], rows_q.at[2], 3, neighbour)
    to_p = send(cols.at[pl.ds(0, n)], cols.at[pl.ds(n, n)], 4, partner)
    to_q1 = send(rows_q.at[0], rows_q.at[1], 5, sibling)

    def score(ci, s):
        logits = dot_nt(cols[ci * n : (ci + 1) * n, :], rows_q[s]) * HEAT
        e = jnp.exp(logits)
        e_t[ci * n : (ci + 1) * n, s * n : (s + 1) * n] = e
        return logits, jnp.sum(e, axis=0, keepdims=True)

    totals = [None] * 4
    logits, totals[0] = score(0, 0)
    eye = lax.broadcasted_iota(jnp.int32, (n, n), 0) == lax.broadcasted_iota(jnp.int32, (n, n), 1)
    positive = jnp.sum(jnp.where(eye, logits, 0.0), axis=0, keepdims=True)
    to_q1.wait_recv()
    totals[1] = score(0, 1)[1]
    to_q.wait_recv()
    to_q3 = send(rows_q.at[2], rows_q.at[3], 6, sibling)
    totals[2] = score(0, 2)[1]
    to_p.wait_recv()
    for s in range(3):
        totals[s] = totals[s] + score(1, s)[1]
    to_q3.wait_recv()
    totals[3] = score(0, 3)[1] + score(1, 3)[1]
    for copy in to_meta:
        copy.wait_recv()

    def z_forward_wait(k, carry):
        @pl.when(2 * k + a - half != 0)
        def _():
            remote(own_row, gathered.at[0, k, a], zf_send.at[k], zf_recv.at[k], sibling).wait_recv()

        return carry

    lax.fori_loop(0, half, z_forward_wait, 0)

    for dx in range(nx):
        for da, yy in ((0, y), (1, y_p)):
            if dx == 0 and da == 0:
                continue
            send(
                gathered.at[0, :, a],
                gathered.at[(nx - dx) % nx, :, a],
                8 + 2 * dx + da,
                at(z, lax.rem(x + dx, nx), yy, c),
            )

    row = lax.broadcasted_iota(jnp.int32, (nb, n), 0)
    row_z = lax.rem(z + lax.rem(row, nz) - half + nz, nz)
    row_x = lax.rem(x + row // nz, nx)
    row_id = (4 * (row_z * nx + row_x) + share).astype(F32)
    named = []
    for s in range(4):
        count = jnp.zeros((nb, n), F32)
        for k in range(7):
            count = count + jnp.where(row_id == meta[s, k : k + 1, :], 1.0, 0.0)
        named.append(count)

    for dx in range(nx):
        for da, aa in ((0, a), (1, 1 - a)):
            if dx or da:
                index = 8 + 2 * dx + da
                landed = gathered.at[(nx - dx) % nx, :, aa]
                remote(landed, landed, send_sem.at[index], recv_sem.at[index], sibling).wait_recv()
    wide[...] = gathered[...].reshape(nb, groups, lanes).astype(F32)
    for j in range(groups):
        cols[2 * n : 2 * n + nb, j * lanes : (j + 1) * lanes] = wide[:, j, :].astype(BF16)
    for s in range(4):
        e = jnp.exp(dot_nt(cols[2 * n : 2 * n + nb, :], rows_q[s]) * HEAT)
        e_t[2 * n : 2 * n + nb, s * n : (s + 1) * n] = e
        sums[0, s : s + 1, :] = totals[s] + jnp.sum(e * named[s], axis=0, keepdims=True)

    to_sums = [send(sums.at[0], sums.at[m], 16 + m, member(m)) for m in (1, 2, 3)]
    for copy in to_sums:
        copy.wait_recv()
    coefs, scaled, loss = [], [], None
    for s in range(4):
        total = sums[0, s : s + 1, :]
        for m in (1, 2, 3):
            total = total + sums[m, s ^ m : (s ^ m) + 1, :]
        if s == 0:
            loss = jnp.log(total) - positive
        weight = meta[s, 7:8, :] * HEAT
        scaled.append(weight)
        coefs.append(weight / total)
    loss_out[...] = loss

    for s in range(4):
        slope = (e_t[2 * n : 2 * n + nb, s * n : (s + 1) * n] * coefs[s]).astype(BF16).astype(F32)
        g_t[2 * n : 2 * n + nb, s * n : (s + 1) * n] = (slope * named[s]).astype(BF16)
    all_q = rows_q[...].reshape(4 * n, depth)
    up = dot_nn(g_t[2 * n : 2 * n + nb, :], all_q)
    for j in range(groups):
        wide[:, j, :] = up[:, j * lanes : (j + 1) * lanes]
    bank_out[...] = wide[...].astype(BF16).reshape(nx, half, 2, groups, lanes)
    to_plane_back = []
    for dx in range(nx):
        for da, (yy, aa) in ((0, (y, a)), (1, (y_p, 1 - a))):
            if dx == 0 and da == 0:
                continue
            to_plane_back.append(
                send(
                    bank_out.at[dx, :, aa],
                    plane_in.at[da, dx],
                    20 + 2 * dx + da,
                    at(z, lax.rem(x + dx, nx), yy, c),
                )
            )

    for s in range(4):
        part = (e_t[n : 2 * n, s * n : (s + 1) * n] * coefs[s]).astype(BF16)
        g_t[n : 2 * n, s * n : (s + 1) * n] = part
    pu_out[...] = dot_nn(g_t[n : 2 * n, :], all_q).astype(BF16)
    for s in range(4):
        part = e_t[0:n, s * n : (s + 1) * n] * coefs[s]
        if s == 0:
            part = part - jnp.where(eye, scaled[0], 0.0)
        g_t[0:n, s * n : (s + 1) * n] = part.astype(BF16)

    for copy in to_plane_back:
        copy.wait_recv()
    total = bank_out[0, :, a].astype(F32)
    for dx in range(nx):
        for da in range(2):
            if dx or da:
                total = total + plane_in[da, dx].astype(F32)
    z_out[...] = total.astype(BF16)

    def z_back(k, carry):
        offset = 2 * k + a - half

        @pl.when(offset != 0)
        def _():
            remote(
                z_out.at[k], z_in.at[k], zb_send.at[k], zb_recv.at[k], at(lax.rem(z + offset + nz, nz), x, y, c)
            ).start()

        return carry

    lax.fori_loop(0, half, z_back, 0)

    @pl.when(a == 0)
    def _():
        z_in[half // 2] = z_out[half // 2]

    to_pu = send(pu_out, pu_in, 28, partner)

    def query_part(s):
        return dot_tn(g_t[:, s * n : (s + 1) * n], cols[...])

    qs_out[0] = query_part(3)
    to_qs3 = send(qs_out.at[0], qs_in.at[0], 29, sibling)
    qs_out[1] = query_part(1)
    to_qs1 = send(qs_out.at[1], qs_in.at[1], 30, sibling)
    mine = query_part(2)
    to_qs3.wait_recv()
    qy_out[...] = (mine + qs_in[0]).astype(BF16)
    to_qy = send(qy_out, qy_in, 31, neighbour)
    passage_up = dot_nn(g_t[0:n, :], all_q)
    to_pu.wait_recv()
    passage_up = passage_up + pu_in[...].astype(F32)
    unit, inv = units(p_raw)
    pg_out[...] = inv * (passage_up - unit * jnp.sum(unit * passage_up, axis=1, keepdims=True))
    query_up = query_part(0)
    to_qs1.wait_recv()
    query_up = query_up + qs_in[1]
    to_qy.wait_recv()
    query_up = query_up + qy_in[...].astype(F32)
    unit, inv = units(q_raw)
    qg_out[...] = inv * (query_up - unit * jnp.sum(unit * query_up, axis=1, keepdims=True))

    def z_back_wait(k, carry):
        @pl.when(2 * k + a - half != 0)
        def _():
            remote(z_out.at[k], z_in.at[k], zb_send.at[k], zb_recv.at[k], sibling).wait_recv()

        return carry

    lax.fori_loop(0, half, z_back_wait, 0)
    g_in[0] = jnp.sum(z_in[...].astype(F32), axis=0)
    to_all = [send(g_in.at[0], g_in.at[m], 32 + m, member(m)) for m in range(1, GROUP)]
    for copy in to_all:
        copy.wait_recv()
    for delta in range(4):
        first, second = [m for m in range(GROUP) if ROW_OF[m] == delta]
        both = g_in[first] + g_in[second]
        row_b = b if delta < 2 else 1 - b
        row_c = 1 - c if delta & 1 else c
        bank_up[2 * row_b + row_c] = both
    up = bank_up[...]
    unit = bank_x[...]
    along = jnp.sum(jnp.sum(unit * up, axis=2, keepdims=True), axis=1, keepdims=True)
    bank_up[...] = bank_inv * (up - unit * along)
    for j in range(groups):
        bg_out[:, j * lanes : (j + 1) * lanes] = bank_up[:, j, :]

    for copy in started:
        copy.wait_send()

    def drain(k, carry):
        @pl.when(2 * k + a - half != 0)
        def _():
            remote(own_row, gathered.at[0, k, a], zf_send.at[k], zf_recv.at[k], sibling).wait_send()
            remote(z_out.at[k], z_in.at[k], zb_send.at[k], zb_recv.at[k], sibling).wait_send()

        return carry

    lax.fori_loop(0, half, drain, 0)


def solution(mesh):
    reps = mesh.shape["rep"]
    nx = NX
    nz = reps // nx

    def body(queries, passages, bank, hard_ids, weights):
        n, depth = queries.shape
        nb = reps
        half = nz // 2
        slab = (depth // 128, 128)
        anywhere = pl.BlockSpec(memory_space=pl.ANY)
        vmem = pl.BlockSpec(memory_space=pltpu.VMEM)
        dma = pltpu.SemaphoreType.DMA
        losses, query_grad, passage_grad, bank_grad = pl.pallas_call(
            functools.partial(kernel, nz, nx),
            out_shape=(
                jax.ShapeDtypeStruct((1, n), F32),
                jax.ShapeDtypeStruct((n, depth), F32),
                jax.ShapeDtypeStruct((n, depth), F32),
                jax.ShapeDtypeStruct((4, depth), F32),
            ),
            in_specs=[anywhere] * 5,
            out_specs=(vmem,) * 4,
            scratch_shapes=[
                pltpu.VMEM((n, depth), BF16),
                pltpu.VMEM((n, depth), BF16),
                pltpu.VMEM((4, depth), BF16),
                pltpu.VMEM((7, n), jnp.int32),
                pltpu.VMEM((1, n), F32),
                pltpu.VMEM((4, n, depth), BF16),
                pltpu.VMEM((2 * n + nb, depth), BF16),
                pltpu.VMEM((4,) + slab, F32),
                pltpu.VMEM(slab, BF16),
                pltpu.VMEM((nx, half, 2) + slab, BF16),
                pltpu.VMEM((nb,) + slab, F32),
                pltpu.VMEM((4, 8, n), F32),
                pltpu.VMEM((4, 8, n), F32),
                pltpu.VMEM((2 * n + nb, 4 * n), F32),
                pltpu.VMEM((2 * n + nb, 4 * n), BF16),
                pltpu.VMEM((nx, half, 2) + slab, BF16),
                pltpu.VMEM((2, nx, half) + slab, BF16),
                pltpu.VMEM((half,) + slab, BF16),
                pltpu.VMEM((half,) + slab, BF16),
                pltpu.VMEM((GROUP,) + slab, F32),
                pltpu.VMEM((4,) + slab, F32),
                pltpu.VMEM((n, depth), BF16),
                pltpu.VMEM((n, depth), BF16),
                pltpu.VMEM((2, n, depth), F32),
                pltpu.VMEM((2, n, depth), F32),
                pltpu.VMEM((n, depth), BF16),
                pltpu.VMEM((n, depth), BF16),
                dma((5,)),
                dma((40,)),
                dma((40,)),
                dma((half,)),
                dma((half,)),
                dma((half,)),
                dma((half,)),
            ],
            compiler_params=pltpu.CompilerParams(
                collective_id=0, has_side_effects=True, vmem_limit_bytes=40 << 20
            ),
        )(queries, passages, bank, hard_ids.T, weights.reshape(1, n))
        return losses.reshape(n), query_grad, passage_grad, bank_grad

    placed = (
        P(("grp", "rep"), None),
        P(("grp", "rep"), None),
        P("rep", None),
        P(("grp", "rep"), None),
        P(("grp", "rep")),
    )
    return jax.shard_map(
        body,
        mesh=mesh,
        in_specs=placed,
        out_specs=(
            P(("grp", "rep")),
            P(("grp", "rep"), None),
            P(("grp", "rep"), None),
            P("rep", None),
        ),
        check_vma=False,
    )
```

time: 895 us -> 83.4 us (0.09)
  waiting for transfers between devices: 804 us -> 0 us
  Pallas kernels: 0 us -> 75.9 us
  blocking collectives: 40.8 us -> 0 us
  between operations: 14.5 us -> 0.65 us
  other arithmetic: 13.2 us -> 0 us
  matrix products: 13.1 us -> 0 us
    unnamed x5 -> x0, waiting for transfers between devices: 490 us -> none
    all_gather x2 -> x0, waiting for transfers between devices: 288 us -> none  [the longest x1 235 us: body(): lax.all_gather(bank_rows, 'rep', axis=0, tiled=True)]
    pallas_call x0 -> x1, Pallas kernels: none -> 75.9 us  [body(): pl.pallas_call(functools.partial(kernel, nz, nx), out_shape=(jax.ShapeDty...]
    psum x1 -> x0, blocking collectives: 40.8 us -> none  [body(): bank_up = lax.psum(owner_part, 'grp')]
    reduce_scatter x1 -> x0, waiting for transfers between devices: 25.7 us -> none  [body(): lax.psum_scatter(passage_terms, 'grp', scatter_dimension=0, tiled=True)]
    dot_general x7 -> x0, matrix products: 13.1 us -> none  [the longest x1 2.82 us: body(): jnp.dot(cohort_logit_slope.T, search_latent_entries, preferred_element_ty...]
  transfers between devices with their start and end apart: 4 -> 0, of which waited for: 4 -> 0; matrix products, arithmetic and copies ran while one was open for 2% -> 0% of each run, Pallas kernels for 0% -> 0%
where the time goes in v1:
time: 83.4 us; the launch traced here: 83.1 us
  Pallas kernels  75.9 us (91%)
  local copies, waits for them, and re-layouts  6.63 us (8%)
    pallas_call x1, Pallas kernels, body(): pl.pallas_call(functools.partial(kernel, nz, nx), out_shape=(jax.ShapeDty...  75.9 us
    unnamed x14, local copies, waits for them, and re-layouts  6.63 us

profile of v1, /device:TPU:1, one launch (start us, length us, event | category | flops | bytes accessed | tf_op | source)
XLA Modules:
  0.0 83.1 jit_solution(6691619429417021359)
XLA Ops:
  0.6 0.0 copy-start.4
  0.6 0.6 copy-done.4
  1.3 0.0 copy-start
  1.3 0.9 %copy-done = bf16[128,1024]{1,0:T(8,128)(2,1)S(1)} copy-done((bf16[128,1024]{1,0:T(8,128)(2,1)S(1)}, bf16[128,1024]{1,0:T(8,128)(2,1)}, u32[]{:S(2)}) %copy-start) | copy-done | bytes 262168
  2.2 0.0 copy-start.1
  2.2 0.9 %copy-done.1 = bf16[128,1024]{1,0:T(8,128)(2,1)S(1)} copy-done((bf16[128,1024]{1,0:T(8,128)(2,1)S(1)}, bf16[128,1024]{1,0:T(8,128)(2,1)}, u32[]{:S(2)}) %copy-start.1) | copy-done | bytes 262168
  3.2 0.0 copy-start.2
  3.2 0.7 copy-done.2
  3.9 0.0 copy-start.3
  3.9 0.7 copy-done.3
  4.6 75.9 %shard_map.84 = (f32[1,128]{1,0:T(1,128)S(1)}, f32[128,1024]{1,0:T(8,128)S(1)}, f32[128,1024]{1,0:T(8,128)S(1)}, f32[4,1024]{1,0:T(4,128)S(1)}) custom-call(bf16[128,1024]{1,0:T(8,128)(2,1)S(1)} %copy-done, bf16[128,1024]{1,0:T(8,128)(2,1)S(1)} %copy-done.1, bf16[4,1024]{1,0:T(4,128)(2,1)S(1)} %copy-done.2, s32[7,128]{1,0:T(8,128)S(1)} %bitcast.3, ...), custom_call_target="tpu_custom_call" | custom-call | tf_op jit(solution)/shard_map/pallas_call | solution.py:418
  80.4 0.5 copy.13
  81.0 0.8 copy.14
  81.7 0.8 copy.15
  82.5 0.6 copy.16
Async XLA Ops:
  0.6 0.7 copy-start.4
  1.3 0.9 %copy-start = (bf16[128,1024]{1,0:T(8,128)(2,1)S(1)}, bf16[128,1024]{1,0:T(8,128)(2,1)}, u32[]{:S(2)}) copy-start(bf16[128,1024]{1,0:T(8,128)(2,1)} %q_in.1) | copy-start | bytes 786436
  2.2 0.9 %copy-start.1 = (bf16[128,1024]{1,0:T(8,128)(2,1)S(1)}, bf16[128,1024]{1,0:T(8,128)(2,1)}, u32[]{:S(2)}) copy-start(bf16[128,1024]{1,0:T(8,128)(2,1)} %p_in.1) | copy-start | bytes 786436
  3.2 0.7 copy-start.2
  3.9 0.7 copy-start.3

commit v2 on v1

v2 whole, which is shorter than its diff:
```python
import functools

import jax
import jax.numpy as jnp
from jax import lax
from jax.experimental import pallas as pl
from jax.experimental.pallas import tpu as pltpu
from jax.sharding import PartitionSpec as P

MESH = pl.DeviceIdType.MESH
F32 = jnp.float32
BF16 = jnp.bfloat16
EPS = 1e-06
HEAT = 20.0
NX = 4
GROUP = 8
ROW_OF = [2 * ((m >> 2 & 1) ^ (m >> 1 & 1)) + (m & 1) for m in range(GROUP)]


def dot_nt(left, right):
    return lax.dot_general(left, right, (((1,), (1,)), ((), ())), preferred_element_type=F32)


def dot_tn(left, right):
    return lax.dot_general(left, right, (((0,), (0,)), ((), ())), preferred_element_type=F32)


def dot_nn(left, right):
    return jnp.dot(left, right, preferred_element_type=F32)


def kernel(
    nz,
    nx,
    q_in,
    p_in,
    bank_in,
    ids_in,
    w_in,
    loss_out,
    qg_out,
    pg_out,
    bg_out,
    q_raw,
    p_raw,
    bank_raw,
    meta_raw,
    w_raw,
    rows_q,
    cols,
    bank_x,
    own_row,
    gathered,
    wide,
    meta,
    sums,
    e_t,
    g_t,
    bank_out,
    plane_in,
    z_out,
    z_in,
    g_in,
    bank_up,
    pu_out,
    pu_in,
    qs_out,
    qs_in,
    qy_out,
    qy_in,
    local_sem,
    send_sem,
    recv_sem,
    zf_send,
    zf_recv,
    zb_send,
    zb_recv,
):
    g, r = lax.axis_index("grp"), lax.axis_index("rep")
    y, c = g // 2, g % 2
    z, x = r // nx, r % nx
    a = y // 2
    b = ((y + 1) // 2) % 2
    share = 2 * b + c
    y_q = y + 1 - 2 * (y % 2)
    y_p = 3 - y
    half, quarter = nz // 2, nz // 4
    n = q_raw.shape[0]
    depth = q_raw.shape[1]
    lanes = 128
    groups = depth // lanes
    nb = nx * nz

    def at(z_, x_, y_, c_):
        return (y_ * 2 + c_, z_ * nx + x_)

    def member(m):
        cc = 1 - c if m & 1 else c
        hi = m >> 1
        yy = (y, y_q, None, y_p)[hi] if hi != 2 else 3 - y_q
        return at(z, x, yy, cc)

    loads = [
        pltpu.make_async_copy(src, dst, local_sem.at[i])
        for i, (src, dst) in enumerate(
            [(bank_in, bank_raw), (q_in, q_raw), (p_in, p_raw), (ids_in, meta_raw), (w_in, w_raw)]
        )
    ]
    for load in loads:
        load.start()

    barrier = pltpu.get_barrier_semaphore()

    def greet(device):
        pl.semaphore_signal(barrier, inc=1, device_id=device, device_id_type=MESH)

    def offset_of(k):
        return 2 * k + a - quarter

    def up_z(offset):
        return at(lax.rem(z + offset + nz, nz), x, y, c)

    greet(up_z(-quarter))

    @pl.when(a == 1)
    def _():
        greet(up_z(quarter))

    def greet_z(k, carry):
        @pl.when(offset_of(k) != 0)
        def _():
            greet(up_z(-offset_of(k)))

        return carry

    lax.fori_loop(0, half // 2, greet_z, 0)
    for dx in range(1, nx):
        for yy in (y, y_p):
            greet(at(z, lax.rem(x + dx, nx), yy, c))
    for m in range(1, GROUP):
        greet(member(m))

    def remote(src, dst, send, recv, device):
        return pltpu.make_async_remote_copy(
            src_ref=src, dst_ref=dst, send_sem=send, recv_sem=recv, device_id=device, device_id_type=MESH
        )

    started = []

    def send(src, dst, index, device):
        copy = remote(src, dst, send_sem.at[index], recv_sem.at[index], device)
        copy.start()
        started.append(copy)
        return copy

    loads[0].wait()
    bank_f = bank_raw[...].astype(F32)
    for j in range(groups):
        bank_x[:, j, :] = bank_f[:, j * lanes : (j + 1) * lanes]
    bank_values = bank_x[...]
    bank_inv = 1.0 / jnp.sqrt(jnp.sum(jnp.sum(bank_values * bank_values, axis=2, keepdims=True), axis=1, keepdims=True) + EPS)
    bank_unit = bank_values * bank_inv
    bank_x[...] = bank_unit
    own_row[...] = bank_x[share].astype(BF16)

    @pl.when(a == 0)
    def _():
        gathered[0, 0, nz // 8, 0] = own_row[...]

    loads[1].wait()
    loads[3].wait()
    loads[4].wait()

    def units(raw):
        values = raw[...].astype(F32)
        inv = 1.0 / jnp.sqrt(jnp.sum(values * values, axis=1, keepdims=True) + EPS)
        return values * inv, inv

    q_unit, q_inv = units(q_raw)
    rows_q[0] = q_unit.astype(BF16)
    meta[0, 0:7, :] = meta_raw[...].astype(F32)
    meta[0, 7:8, :] = w_raw[...]
    loads[2].wait()
    p_unit, p_inv = units(p_raw)
    cols[0:n, :] = p_unit.astype(BF16)

    pl.semaphore_wait(barrier, half // 2 + 2 * a + 2 * (nx - 1) + GROUP - 1)

    def z_copy(k, device):
        return remote(own_row, gathered.at[0, 0, k, a], zf_send.at[k], zf_recv.at[k], device)

    def z_forward(k, carry):
        @pl.when(offset_of(k) != 0)
        def _():
            z_copy(k, up_z(-offset_of(k))).start()

        return carry

    lax.fori_loop(0, half // 2, z_forward, 0)

    sibling = member(1)
    neighbour = member(2)
    partner = member(6)
    to_meta = [send(meta.at[0], meta.at[m], m - 1, member(m)) for m in (1, 2, 3)]
    to_q = send(rows_q.at[0], rows_q.at[2], 3, neighbour)
    to_p = send(cols.at[pl.ds(0, n)], cols.at[pl.ds(n, n)], 4, partner)
    to_q1 = send(rows_q.at[0], rows_q.at[1], 5, sibling)

    def score(ci, s):
        logits = dot_nt(cols[ci * n : (ci + 1) * n, :], rows_q[s]) * HEAT
        e = jnp.exp(logits)
        e_t[ci * n : (ci + 1) * n, s * n : (s + 1) * n] = e
        return logits, jnp.sum(e, axis=0, keepdims=True)

    def z_forward_wait(k, carry):
        @pl.when(offset_of(k) != 0)
        def _():
            z_copy(k, sibling).wait_recv()

        return carry

    def to_plane(part):
        for dx in (2, 1, 3) if nx == 4 else range(1, nx):
            for da, yy in ((0, y), (1, y_p)):
                send(
                    gathered.at[part, 0, :, a],
                    gathered.at[part, (nx - dx) % nx, :, a],
                    8 + 8 * part + 2 * dx + da,
                    at(z, lax.rem(x + dx, nx), yy, c),
                )
        send(gathered.at[part, 0, :, a], gathered.at[part, 0, :, a], 8 + 8 * part + 1, partner)

    def from_plane(part):
        for dx in range(nx):
            for da, aa in ((0, a), (1, 1 - a)):
                if dx or da:
                    index = 8 + 8 * part + 2 * dx + da
                    landed = gathered.at[part, (nx - dx) % nx, :, aa]
                    remote(landed, landed, send_sem.at[index], recv_sem.at[index], sibling).wait_recv()

    totals = [None] * 4
    logits, totals[0] = score(0, 0)
    eye = lax.broadcasted_iota(jnp.int32, (n, n), 0) == lax.broadcasted_iota(jnp.int32, (n, n), 1)
    positive = jnp.sum(jnp.where(eye, logits, 0.0), axis=0, keepdims=True)
    to_q1.wait_recv()
    totals[1] = score(0, 1)[1]
    lax.fori_loop(0, half // 2, z_forward_wait, 0)
    eighth = nz // 8
    low, high = pl.ds(0, eighth), pl.ds(eighth, eighth)
    to_high = send(gathered.at[0, 0, low, a], gathered.at[1, 0, high, a], 28, up_z(quarter))
    to_low = send(gathered.at[0, 0, high, a], gathered.at[1, 0, low, a], 29, up_z(-quarter))
    to_plane(0)

    to_q.wait_recv()
    to_q3 = send(rows_q.at[2], rows_q.at[3], 6, sibling)
    totals[2] = score(0, 2)[1]
    to_p.wait_recv()
    for s in range(3):
        totals[s] = totals[s] + score(1, s)[1]
    to_q3.wait_recv()
    totals[3] = score(0, 3)[1] + score(1, 3)[1]
    for copy in to_meta:
        copy.wait_recv()

    hb = nb // 2
    all_q = rows_q[...].reshape(4 * n, depth)

    def bank_score(part):
        first = 2 * n + part * hb
        wide[part * hb : (part + 1) * hb] = gathered[part].reshape(hb, groups, lanes).astype(F32)
        for j in range(groups):
            cols[first : first + hb, j * lanes : (j + 1) * lanes] = wide[part * hb : (part + 1) * hb, j, :].astype(BF16)
        e = jnp.exp(dot_nt(cols[first : first + hb, :], all_q) * HEAT)
        e_t[first : first + hb, :] = e
        return [jnp.sum(e[:, s * n : (s + 1) * n] * named[part][s], axis=0, keepdims=True) for s in range(4)]

    named = []
    for part in range(2):
        row = lax.broadcasted_iota(jnp.int32, (hb, n), 0)
        row_z = lax.rem(z + part * half + lax.rem(row, half) - quarter + nz, nz)
        row_x = lax.rem(x + row // half, nx)
        row_id = (4 * (row_z * nx + row_x) + share).astype(F32)
        counts = []
        for s in range(4):
            count = jnp.zeros((hb, n), F32)
            for k in range(7):
                count = count + jnp.where(row_id == meta[s, k : k + 1, :], 1.0, 0.0)
            counts.append(count)
        named.append(counts)

    from_plane(0)
    near = bank_score(0)
    to_high.wait_recv()
    to_low.wait_recv()
    to_plane(1)
    from_plane(1)
    far = bank_score(1)
    for s in range(4):
        sums[0, s : s + 1, :] = totals[s] + near[s] + far[s]

    to_sums = [send(sums.at[0], sums.at[m], 24 + m, member(m)) for m in (2, 3, 1)]
    for copy in to_sums:
        copy.wait_recv()
    coefs, scaled = [], []
    for s in range(4):
        total = sums[0, s : s + 1, :]
        for m in (1, 2, 3):
            total = total + sums[m, s ^ m : (s ^ m) + 1, :]
        if s == 0:
            loss_out[...] = jnp.log(total) - positive
        weight = meta[s, 7:8, :] * HEAT
        scaled.append(weight)
        coefs.append(weight / total)

    def bank_slopes(part):
        first, rows = 2 * n + part * hb, slice(part * hb, (part + 1) * hb)
        for s in range(4):
            slope = (e_t[first : first + hb, s * n : (s + 1) * n] * coefs[s]).astype(BF16).astype(F32)
            g_t[first : first + hb, s * n : (s + 1) * n] = (slope * named[part][s]).astype(BF16)
        up = dot_nn(g_t[first : first + hb, :], all_q)
        for j in range(groups):
            wide[rows, j, :] = up[:, j * lanes : (j + 1) * lanes]
        bank_out[part] = wide[rows].astype(BF16).reshape(nx, half // 2, 2, groups, lanes)
        copies = []
        for dx in (2, 1, 3, 0) if nx == 4 else range(nx):
            for da, (yy, aa) in ((0, (y, a)), (1, (y_p, 1 - a))):
                if dx or da:
                    copies.append(
                        send(
                            bank_out.at[part, dx, :, aa],
                            plane_in.at[part, da, dx],
                            48 + 8 * part + 2 * dx + da,
                            at(z, lax.rem(x + dx, nx), yy, c),
                        )
                    )
        return copies

    to_back = [None, bank_slopes(1)]
    to_back[0] = bank_slopes(0)

    for s in range(4):
        part = (e_t[n : 2 * n, s * n : (s + 1) * n] * coefs[s]).astype(BF16)
        g_t[n : 2 * n, s * n : (s + 1) * n] = part
    pu_out[...] = dot_nn(g_t[n : 2 * n, :], all_q).astype(BF16)
    for s in range(4):
        part = e_t[0:n, s * n : (s + 1) * n] * coefs[s]
        if s == 0:
            part = part - jnp.where(eye, scaled[0], 0.0)
        g_t[0:n, s * n : (s + 1) * n] = part.astype(BF16)

    def query_part(s):
        return dot_tn(g_t[:, s * n : (s + 1) * n], cols[...])

    qs_out[0] = query_part(3)
    to_qs3 = send(qs_out.at[0], qs_in.at[0], 37, sibling)
    qs_out[1] = query_part(1)
    to_qs1 = send(qs_out.at[1], qs_in.at[1], 38, sibling)

    def z_back_copy(k, device):
        return remote(z_out.at[k], z_in.at[k], zb_send.at[k], zb_recv.at[k], device)

    def z_back(k):
        @pl.when(offset_of(k) != 0)
        def _():
            z_back_copy(k, up_z(offset_of(k))).start()

    def z_back_far(i, carry):
        z_back(3 * nz // 8 + (1 - 2 * lax.rem(i, 2)) * ((i + 1) // 2))
        return carry

    def z_back_near(i, carry):
        z_back(i)
        return carry

    def bank_reduce(part):
        for copy in to_back[part]:
            copy.wait_recv()
        total = bank_out[part, 0, :, a].astype(F32)
        for dx in range(nx):
            for da in range(2):
                if dx or da:
                    total = total + plane_in[part, da, dx].astype(F32)
        z_out[part * (half // 2) : (part + 1) * (half // 2)] = total.astype(BF16)
        lax.fori_loop(0, half // 2, z_back_far if part else z_back_near, 0)

    bank_reduce(1)
    bank_reduce(0)

    @pl.when(a == 0)
    def _():
        z_in[nz // 8] = z_out[nz // 8]

    to_pu = send(pu_out, pu_in, 36, partner)

    mine = query_part(2)
    to_qs3.wait_recv()
    qy_out[...] = (mine + qs_in[0]).astype(BF16)
    to_qy = send(qy_out, qy_in, 39, neighbour)
    passage_up = dot_nn(g_t[0:n, :], all_q)
    to_pu.wait_recv()
    passage_up = passage_up + pu_in[...].astype(F32)
    unit, inv = units(p_raw)
    pg_out[...] = inv * (passage_up - unit * jnp.sum(unit * passage_up, axis=1, keepdims=True))
    query_up = query_part(0)
    to_qs1.wait_recv()
    query_up = query_up + qs_in[1]
    to_qy.wait_recv()
    query_up = query_up + qy_in[...].astype(F32)
    unit, inv = units(q_raw)
    qg_out[...] = inv * (query_up - unit * jnp.sum(unit * query_up, axis=1, keepdims=True))

    for copy in started:
        copy.wait_send()

    def drain(k, carry):
        @pl.when(offset_of(k) != 0)
        def _():
            z_back_copy(k, sibling).wait_send()

        return carry

    def drain_forward(k, carry):
        @pl.when(offset_of(k) != 0)
        def _():
            z_copy(k, sibling).wait_send()

        return carry

    lax.fori_loop(0, half, drain, 0)
    lax.fori_loop(0, half // 2, drain_forward, 0)

    def z_back_wait(k, carry):
        @pl.when(offset_of(k) != 0)
        def _():
            z_back_copy(k, sibling).wait_recv()

        return carry

    lax.fori_loop(0, half, z_back_wait, 0)
    g_in[0] = jnp.sum(z_in[...].astype(F32), axis=0)
    to_all = [send(g_in.at[0], g_in.at[m], 40 + m, member(m)) for m in (5, 4, 7, 6, 3, 2, 1)]
    for copy in to_all:
        copy.wait_recv()
    for delta in range(4):
        first, second = [m for m in range(GROUP) if ROW_OF[m] == delta]
        both = g_in[first] + g_in[second]
        row_b = b if delta < 2 else 1 - b
        row_c = 1 - c if delta & 1 else c
        bank_up[2 * row_b + row_c] = both
    up = bank_up[...]
    unit = bank_x[...]
    along = jnp.sum(jnp.sum(unit * up, axis=2, keepdims=True), axis=1, keepdims=True)
    bank_up[...] = bank_inv * (up - unit * along)
    for j in range(groups):
        bg_out[:, j * lanes : (j + 1) * lanes] = bank_up[:, j, :]
    for copy in to_all:
        copy.wait_send()


def hand_over(*refs):
    count = (len(refs) - 1) // 2
    sems = refs[-1]
    copies = [pltpu.make_async_copy(refs[i], refs[count + i], sems.at[i]) for i in range(count)]
    for copy in copies:
        copy.start()
    for copy in copies:
        copy.wait()


def solution(mesh):
    reps = mesh.shape["rep"]
    nx = NX
    nz = reps // nx

    def body(queries, passages, bank, hard_ids, weights):
        n, depth = queries.shape
        nb = reps
        half = nz // 2
        slab = (depth // 128, 128)
        hbm = pl.BlockSpec(memory_space=pltpu.HBM)
        vmem = pl.BlockSpec(memory_space=pltpu.VMEM)
        dma = pltpu.SemaphoreType.DMA
        results = (
            jax.ShapeDtypeStruct((1, n), F32),
            jax.ShapeDtypeStruct((n, depth), F32),
            jax.ShapeDtypeStruct((n, depth), F32),
            jax.ShapeDtypeStruct((4, depth), F32),
        )
        given = [
            pltpu.with_memory_space_constraint(value, pltpu.HBM)
            for value in (queries, passages, bank, hard_ids.T, weights.reshape(1, n))
        ]
        made = pl.pallas_call(
            functools.partial(kernel, nz, nx),
            out_shape=results,
            in_specs=[hbm] * 5,
            out_specs=(vmem,) * 4,
            scratch_shapes=[
                pltpu.VMEM((n, depth), BF16),
                pltpu.VMEM((n, depth), BF16),
                pltpu.VMEM((4, depth), BF16),
                pltpu.VMEM((7, n), jnp.int32),
                pltpu.VMEM((1, n), F32),
                pltpu.VMEM((4, n, depth), BF16),
                pltpu.VMEM((2 * n + nb, depth), BF16),
                pltpu.VMEM((4,) + slab, F32),
                pltpu.VMEM(slab, BF16),
                pltpu.VMEM((2, nx, half // 2, 2) + slab, BF16),
                pltpu.VMEM((nb,) + slab, F32),
                pltpu.VMEM((4, 8, n), F32),
                pltpu.VMEM((4, 8, n), F32),
                pltpu.VMEM((2 * n + nb, 4 * n), F32),
                pltpu.VMEM((2 * n + nb, 4 * n), BF16),
                pltpu.VMEM((2, nx, half // 2, 2) + slab, BF16),
                pltpu.VMEM((2, 2, nx, half // 2) + slab, BF16),
                pltpu.VMEM((half,) + slab, BF16),
                pltpu.VMEM((half,) + slab, BF16),
                pltpu.VMEM((GROUP,) + slab, F32),
                pltpu.VMEM((4,) + slab, F32),
                pltpu.VMEM((n, depth), BF16),
                pltpu.VMEM((n, depth), BF16),
                pltpu.VMEM((2, n, depth), F32),
                pltpu.VMEM((2, n, depth), F32),
                pltpu.VMEM((n, depth), BF16),
                pltpu.VMEM((n, depth), BF16),
                dma((5,)),
                dma((64,)),
                dma((64,)),
                dma((half // 2,)),
                dma((half // 2,)),
                dma((half,)),
                dma((half,)),
            ],
            compiler_params=pltpu.CompilerParams(
                collective_id=0, has_side_effects=True, vmem_limit_bytes=40 << 20
            ),
        )(*given)
        losses, query_grad, passage_grad, bank_grad = pl.pallas_call(
            hand_over,
            out_shape=results,
            in_specs=[vmem] * 4,
            out_specs=(hbm,) * 4,
            scratch_shapes=[dma((4,))],
        )(*made)
        return losses.reshape(n), query_grad, passage_grad, bank_grad

    placed = (
        P(("grp", "rep"), None),
        P(("grp", "rep"), None),
        P("rep", None),
        P(("grp", "rep"), None),
        P(("grp", "rep")),
    )
    return jax.shard_map(
        body,
        mesh=mesh,
        in_specs=placed,
        out_specs=(
            P(("grp", "rep")),
            P(("grp", "rep"), None),
            P(("grp", "rep"), None),
            P("rep", None),
        ),
        check_vma=False,
    )
```

time: 83.4 us -> 74.5 us (0.89)
  Pallas kernels: 75.9 us -> 70.9 us
  local copies, waits for them, and re-layouts: 6.63 us -> 2.71 us
    pallas_call x1 -> x2, Pallas kernels: 75.9 us -> 70.9 us  [the longest x1 68.7 us: body(): pl.pallas_call(functools.partial(kernel, nz, nx), out_shape=results, in_s...]
    unnamed x14 -> x8, local copies, waits for them, and re-layouts: 6.63 us -> 2.71 us
where the time goes in v2:
time: 74.5 us; the launch traced here: 74.3 us
  Pallas kernels  70.9 us (95%)
  local copies, waits for them, and re-layouts  2.71 us (4%)
    pallas_call x1, Pallas kernels, body(): pl.pallas_call(functools.partial(kernel, nz, nx), out_shape=results, in_s...  68.7 us
    unnamed x8, local copies, waits for them, and re-layouts  2.71 us
    pallas_call x1, Pallas kernels, body(): pl.pallas_call(hand_over, out_shape=results, in_specs=[vmem] * 4, out_spe...  2.21 us

profile of v2, /device:TPU:1, one launch (start us, length us, event | category | flops | bytes accessed | tf_op | source)
XLA Modules:
  0.0 74.3 jit_solution(14478743727416710307)
XLA Ops:
  0.6 68.7 %shard_map.84 = (f32[1,128]{1,0:T(1,128)S(1)}, f32[128,1024]{1,0:T(8,128)S(1)}, f32[128,1024]{1,0:T(8,128)S(1)}, f32[4,1024]{1,0:T(4,128)S(1)}) custom-call(bf16[128,1024]{1,0:T(8,128)(2,1)} %q_in.1, bf16[128,1024]{1,0:T(8,128)(2,1)} %p_in.1, bf16[4,1024]{1,0:T(4,128)(2,1)} %bank_in.1, s32[7,128]{1,0:T(8,128)} %bitcast.3, f32[1,128]{1,0:T(1,128)} %bitcast.4), custom_call_target="tpu_custom_call" | custom-call | tf_op jit(solution)/shard_map/pallas_call | solution.py:493
  69.4 0.0 copy-start
  69.4 0.8 %copy-done = f32[128,1024]{1,0:T(8,128)} copy-done((f32[128,1024]{1,0:T(8,128)}, f32[128,1024]{1,0:T(8,128)S(1)}, u32[]{:S(2)}) %copy-start) | copy-done | bytes 524312
  70.1 0.0 copy-start.1
  70.1 0.8 %copy-done.1 = f32[128,1024]{1,0:T(8,128)} copy-done((f32[128,1024]{1,0:T(8,128)}, f32[128,1024]{1,0:T(8,128)S(1)}, u32[]{:S(2)}) %copy-start.1) | copy-done | bytes 524312
  70.9 0.0 copy-start.2
  70.9 0.6 copy-done.2
  71.5 0.0 copy-start.3
  71.5 0.5 copy-done.3
  72.1 2.2 %shard_map.85 = (f32[1,128]{1,0:T(1,128)}, f32[128,1024]{1,0:T(8,128)}, f32[128,1024]{1,0:T(8,128)}, f32[4,1024]{1,0:T(4,128)}) custom-call(f32[1,128]{1,0:T(1,128)} %copy-done.3, f32[128,1024]{1,0:T(8,128)} %copy-done, f32[128,1024]{1,0:T(8,128)} %copy-done.1, f32[4,1024]{1,0:T(4,128)} %copy-done.2), custom_call_target="tpu_custom_call" | custom-call | tf_op jit(solution)/shard_map/pallas_call | solution.py:538
Async XLA Ops:
  69.4 0.8 %copy-start = (f32[128,1024]{1,0:T(8,128)}, f32[128,1024]{1,0:T(8,128)S(1)}, u32[]{:S(2)}) copy-start(f32[128,1024]{1,0:T(8,128)S(1)} %get-tuple-element.13.refs_1_) | copy-start | bytes 1572868
  70.1 0.8 %copy-start.1 = (f32[128,1024]{1,0:T(8,128)}, f32[128,1024]{1,0:T(8,128)S(1)}, u32[]{:S(2)}) copy-start(f32[128,1024]{1,0:T(8,128)S(1)} %get-tuple-element.14.refs_2_) | copy-start | bytes 1572868
  70.9 0.6 copy-start.2
  71.5 0.5 copy-start.3

commit v3 on v2

--- a/solution.py
+++ b/solution.py
@@ -100,6 +100,37 @@
         yy = (y, y_q, None, y_p)[hi] if hi != 2 else 3 - y_q
         return at(z, x, yy, cc)
 
+    barrier = pltpu.get_barrier_semaphore()
+
+    def greet(device):
+        pl.semaphore_signal(barrier, inc=1, device_id=device, device_id_type=MESH)
+
+    def offset_of(k):
+        return 2 * k + a - quarter
+
+    def up_z(offset):
+        return at(lax.rem(z + offset + nz, nz), x, y, c)
+
+    greet(up_z(-quarter))
+
+    @pl.when(a == 1)
+    def _():
+        greet(up_z(quarter))
+
+    def greet_z(k, carry):
+        @pl.when(offset_of(k) != 0)
+        def _():
+            greet(up_z(-offset_of(k)))
+
+        return carry
+
+    lax.fori_loop(0, half // 2, greet_z, 0)
+    for dx in range(1, nx):
+        for yy in (y, y_p):
+            greet(at(z, lax.rem(x + dx, nx), yy, c))
+    for m in range(1, GROUP):
+        greet(member(m))
+
     loads = [
         pltpu.make_async_copy(src, dst, local_sem.at[i])
         for i, (src, dst) in enumerate(
@@ -108,37 +139,6 @@
     ]
     for load in loads:
         load.start()
-
-    barrier = pltpu.get_barrier_semaphore()
-
-    def greet(device):
-        pl.semaphore_signal(barrier, inc=1, device_id=device, device_id_type=MESH)
-
-    def offset_of(k):
-        return 2 * k + a - quarter
-
-    def up_z(offset):
-        return at(lax.rem(z + offset + nz, nz), x, y, c)
-
-    greet(up_z(-quarter))
-
-    @pl.when(a == 1)
-    def _():
-        greet(up_z(quarter))
-
-    def greet_z(k, carry):
-        @pl.when(offset_of(k) != 0)
-        def _():
-            greet(up_z(-offset_of(k)))
-
-        return carry
-
-    lax.fori_loop(0, half // 2, greet_z, 0)
-    for dx in range(1, nx):
-        for yy in (y, y_p):
-            greet(at(z, lax.rem(x + dx, nx), yy, c))
-    for m in range(1, GROUP):
-        greet(member(m))
 
     def remote(src, dst, send, recv, device):
         return pltpu.make_async_remote_copy(
@@ -541,6 +541,7 @@
             in_specs=[vmem] * 4,
             out_specs=(hbm,) * 4,
             scratch_shapes=[dma((4,))],
+            compiler_params=pltpu.CompilerParams(vmem_limit_bytes=1 << 20),
         )(*made)
         return losses.reshape(n), query_grad, passage_grad, bank_grad
 

time: 74.5 us -> 70.5 us (0.946)
  local copies, waits for them, and re-layouts: 2.71 us -> 0 us
  Pallas kernels: 70.9 us -> 69.7 us
    unnamed x8 -> x0, local copies, waits for them, and re-layouts: 2.71 us -> none
    pallas_call x1, Pallas kernels: 2.21 us -> 1.01 us  [body(): pl.pallas_call(hand_over, out_shape=results, in_specs=[vmem] * 4, out_spe...]
where the time goes in v3:
time: 70.5 us; the launch traced here: 70.4 us
  Pallas kernels  69.7 us (99%)
    pallas_call x1, Pallas kernels, body(): pl.pallas_call(functools.partial(kernel, nz, nx), out_shape=results, in_s...  68.7 us

profile of v3, /device:TPU:1, one launch (start us, length us, event | category | flops | bytes accessed | tf_op | source)
XLA Modules:
  0.0 70.4 jit_solution(16157960783503526009)
XLA Ops:
  0.6 68.7 %shard_map.84 = (f32[1,128]{1,0:T(1,128)S(1)}, f32[128,1024]{1,0:T(8,128)S(1)}, f32[128,1024]{1,0:T(8,128)S(1)}, f32[4,1024]{1,0:T(4,128)S(1)}) custom-call(bf16[128,1024]{1,0:T(8,128)(2,1)} %q_in.1, bf16[128,1024]{1,0:T(8,128)(2,1)} %p_in.1, bf16[4,1024]{1,0:T(4,128)(2,1)} %bank_in.1, s32[7,128]{1,0:T(8,128)} %bitcast.3, f32[1,128]{1,0:T(1,128)} %bitcast.4), custom_call_target="tpu_custom_call" | custom-call | tf_op jit(solution)/shard_map/pallas_call | solution.py:493
  69.3 1.0 %shard_map.85 = (f32[1,128]{1,0:T(1,128)}, f32[128,1024]{1,0:T(8,128)}, f32[128,1024]{1,0:T(8,128)}, f32[4,1024]{1,0:T(4,128)}) custom-call(f32[1,128]{1,0:T(1,128)S(1)} %get-tuple-element.12.refs_0_, f32[128,1024]{1,0:T(8,128)S(1)} %get-tuple-element.13.refs_1_, f32[128,1024]{1,0:T(8,128)S(1)} %get-tuple-element.14.refs_2_, ...), custom_call_target="tpu_custom_call" | custom-call | tf_op jit(solution)/shard_map/pallas_call | solution.py:538

commit v4 on v3

--- a/solution.py
+++ b/solution.py
@@ -40,7 +40,9 @@
     loss_out,
     qg_out,
     pg_out,
-    bg_out,
+    up_out,
+    unit_out,
+    inv_out,
     q_raw,
     p_raw,
     bank_raw,
@@ -61,7 +63,6 @@
     z_out,
     z_in,
     g_in,
-    bank_up,
     pu_out,
     pu_in,
     qs_out,
@@ -307,7 +308,7 @@
         for m in (1, 2, 3):
             total = total + sums[m, s ^ m : (s ^ m) + 1, :]
         if s == 0:
-            loss_out[...] = jnp.log(total) - positive
+            own_total = total
         weight = meta[s, 7:8, :] * HEAT
         scaled.append(weight)
         coefs.append(weight / total)
@@ -338,6 +339,8 @@
     to_back = [None, bank_slopes(1)]
     to_back[0] = bank_slopes(0)
 
+    loss_out[...] = jnp.log(own_total) - positive
+
     for s in range(4):
         part = (e_t[n : 2 * n, s * n : (s + 1) * n] * coefs[s]).astype(BF16)
         g_t[n : 2 * n, s * n : (s + 1) * n] = part
@@ -359,17 +362,11 @@
     def z_back_copy(k, device):
         return remote(z_out.at[k], z_in.at[k], zb_send.at[k], zb_recv.at[k], device)
 
-    def z_back(k):
+    def z_back_near(k, carry):
         @pl.when(offset_of(k) != 0)
         def _():
             z_back_copy(k, up_z(offset_of(k))).start()
 
-    def z_back_far(i, carry):
-        z_back(3 * nz // 8 + (1 - 2 * lax.rem(i, 2)) * ((i + 1) // 2))
-        return carry
-
-    def z_back_near(i, carry):
-        z_back(i)
         return carry
 
     def bank_reduce(part):
@@ -381,7 +378,12 @@
                 if dx or da:
                     total = total + plane_in[part, da, dx].astype(F32)
         z_out[part * (half // 2) : (part + 1) * (half // 2)] = total.astype(BF16)
-        lax.fori_loop(0, half // 2, z_back_far if part else z_back_near, 0)
+        if part:
+            for i in range(half // 2):
+                k = 3 * nz // 8 + (1 - 2 * (i % 2)) * ((i + 1) // 2)
+                z_back_copy(k, up_z(offset_of(k))).start()
+        else:
+            lax.fori_loop(0, half // 2, z_back_near, 0)
 
     bank_reduce(1)
     bank_reduce(0)
@@ -409,6 +411,9 @@
     unit, inv = units(q_raw)
     qg_out[...] = inv * (query_up - unit * jnp.sum(unit * query_up, axis=1, keepdims=True))
 
+    unit_out[...] = bank_x[...]
+    inv_out[...] = jnp.broadcast_to(bank_inv, inv_out.shape)
+
     for copy in started:
         copy.wait_send()
 
@@ -446,25 +451,26 @@
         both = g_in[first] + g_in[second]
         row_b = b if delta < 2 else 1 - b
         row_c = 1 - c if delta & 1 else c
-        bank_up[2 * row_b + row_c] = both
-    up = bank_up[...]
-    unit = bank_x[...]
-    along = jnp.sum(jnp.sum(unit * up, axis=2, keepdims=True), axis=1, keepdims=True)
-    bank_up[...] = bank_inv * (up - unit * along)
-    for j in range(groups):
-        bg_out[:, j * lanes : (j + 1) * lanes] = bank_up[:, j, :]
+        up_out[2 * row_b + row_c] = both
     for copy in to_all:
         copy.wait_send()
 
 
-def hand_over(*refs):
-    count = (len(refs) - 1) // 2
-    sems = refs[-1]
-    copies = [pltpu.make_async_copy(refs[i], refs[count + i], sems.at[i]) for i in range(count)]
+def finish(loss, qg, pg, up_ref, unit_ref, inv_ref, loss_out, qg_out, pg_out, bg_out, slabs, rows, sems):
+    copies = [pltpu.make_async_copy(loss, loss_out, sems.at[0])]
+    copies += [pltpu.make_async_copy(qg, qg_out, sems.at[1]), pltpu.make_async_copy(pg, pg_out, sems.at[2])]
     for copy in copies:
         copy.start()
+    up, unit = up_ref[...], unit_ref[...]
+    along = jnp.sum(jnp.sum(unit * up, axis=2, keepdims=True), axis=1, keepdims=True)
+    slabs[...] = inv_ref[...] * (up - unit * along)
+    for j in range(slabs.shape[1]):
+        rows[:, j * 128 : (j + 1) * 128] = slabs[:, j, :]
+    last = pltpu.make_async_copy(rows, bg_out, sems.at[3])
+    last.start()
     for copy in copies:
         copy.wait()
+    last.wait()
 
 
 def solution(mesh):
@@ -484,17 +490,17 @@
             jax.ShapeDtypeStruct((1, n), F32),
             jax.ShapeDtypeStruct((n, depth), F32),
             jax.ShapeDtypeStruct((n, depth), F32),
-            jax.ShapeDtypeStruct((4, depth), F32),
         )
+        small = jax.ShapeDtypeStruct((4,) + slab, F32)
         given = [
             pltpu.with_memory_space_constraint(value, pltpu.HBM)
             for value in (queries, passages, bank, hard_ids.T, weights.reshape(1, n))
         ]
         made = pl.pallas_call(
             functools.partial(kernel, nz, nx),
-            out_shape=results,
+            out_shape=results + (small,) * 3,
             in_specs=[hbm] * 5,
-            out_specs=(vmem,) * 4,
+            out_specs=(vmem,) * 6,
             scratch_shapes=[
                 pltpu.VMEM((n, depth), BF16),
                 pltpu.VMEM((n, depth), BF16),
@@ -516,7 +522,6 @@
                 pltpu.VMEM((half,) + slab, BF16),
                 pltpu.VMEM((half,) + slab, BF16),
                 pltpu.VMEM((GROUP,) + slab, F32),
-                pltpu.VMEM((4,) + slab, F32),
                 pltpu.VMEM((n, depth), BF16),
                 pltpu.VMEM((n, depth), BF16),
                 pltpu.VMEM((2, n, depth), F32),
@@ -536,11 +541,11 @@
             ),
         )(*given)
         losses, query_grad, passage_grad, bank_grad = pl.pallas_call(
-            hand_over,
-            out_shape=results,
-            in_specs=[vmem] * 4,
+            finish,
+            out_shape=results + (jax.ShapeDtypeStruct((4, depth), F32),),
+            in_specs=[vmem] * 6,
             out_specs=(hbm,) * 4,
-            scratch_shapes=[dma((4,))],
+            scratch_shapes=[pltpu.VMEM((4,) + slab, F32), pltpu.VMEM((4, depth), F32), dma((4,))],
             compiler_params=pltpu.CompilerParams(vmem_limit_bytes=1 << 20),
         )(*made)
         return losses.reshape(n), query_grad, passage_grad, bank_grad

time: 70.5 us -> 70.4 us (level)
  no operation moved by 1% of the time
where the time goes in v4:
time: 70.4 us; the launch traced here: 70.2 us
  Pallas kernels  69.6 us (99%)
    pallas_call x1, Pallas kernels, body(): pl.pallas_call(functools.partial(kernel, nz, nx), out_shape=results + (sm...  68.6 us

profile of v4, /device:TPU:1, one launch (start us, length us, event | category | flops | bytes accessed | tf_op | source)
XLA Modules:
  0.0 70.2 jit_solution(10188335110340000673)
XLA Ops:
  0.6 68.6 %shard_map.84 = (f32[1,128]{1,0:T(1,128)S(1)}, f32[128,1024]{1,0:T(8,128)S(1)}, f32[128,1024]{1,0:T(8,128)S(1)}, f32[4,8,128]{2,1,0:T(8,128)S(1)}, f32[4,8,128]{2,1,0:T(8,128)S(1)}, /*index=5*/f32[4,8,128]{2,1,0:T(8,128)S(1)}) custom-call(bf16[128,1024]{1,0:T(8,128)(2,1)} %q_in.1, bf16[128,1024]{1,0:T(8,128)(2,1)} %p_in.1, bf16[4,1024]{1,0:T(4,128)(2,1)} %bank_in.1, ...), custom_call_target="tpu_custom_call" | custom-call | tf_op jit(solution)/shard_map/pallas_call | solution.py:499
  69.2 1.0 %shard_map.85 = (f32[1,128]{1,0:T(1,128)}, f32[128,1024]{1,0:T(8,128)}, f32[128,1024]{1,0:T(8,128)}, f32[4,1024]{1,0:T(4,128)}) custom-call(f32[1,128]{1,0:T(1,128)S(1)} %get-tuple-element.14.loss, f32[128,1024]{1,0:T(8,128)S(1)} %get-tuple-element.15.qg, f32[128,1024]{1,0:T(8,128)S(1)} %get-tuple-element.16.pg, f32[4,8,128]{2,1,0:T(8,128)S(1)} %get-tuple-element.17.up_ref, ...), custom_call_target="tpu_custom_call" | custom-call | tf_op jit(solution)/shard_map/pallas_call | solution.py:543

commit v5 on v4

--- a/solution.py
+++ b/solution.py
@@ -220,9 +220,13 @@
 
         return carry
 
+    plane_order = [(dx, da) for dx in range(nx) for da in range(2) if dx or da]
+    plane_order.sort(key=lambda at_: -(min(at_[0], nx - at_[0]) + at_[1]))
+
     def to_plane(part):
-        for dx in (2, 1, 3) if nx == 4 else range(1, nx):
-            for da, yy in ((0, y), (1, y_p)):
+        for dx, da in plane_order:
+            if dx:
+                yy = y_p if da else y
                 send(
                     gathered.at[part, 0, :, a],
                     gathered.at[part, (nx - dx) % nx, :, a],
@@ -323,17 +327,16 @@
             wide[rows, j, :] = up[:, j * lanes : (j + 1) * lanes]
         bank_out[part] = wide[rows].astype(BF16).reshape(nx, half // 2, 2, groups, lanes)
         copies = []
-        for dx in (2, 1, 3, 0) if nx == 4 else range(nx):
-            for da, (yy, aa) in ((0, (y, a)), (1, (y_p, 1 - a))):
-                if dx or da:
-                    copies.append(
-                        send(
-                            bank_out.at[part, dx, :, aa],
-                            plane_in.at[part, da, dx],
-                            48 + 8 * part + 2 * dx + da,
-                            at(z, lax.rem(x + dx, nx), yy, c),
-                        )
-                    )
+        for dx, da in plane_order:
+            yy, aa = (y_p, 1 - a) if da else (y, a)
+            copies.append(
+                send(
+                    bank_out.at[part, dx, :, aa],
+                    plane_in.at[part, da, dx],
+                    48 + 8 * part + 2 * dx + da,
+                    at(z, lax.rem(x + dx, nx), yy, c),
+                )
+            )
         return copies
 
     to_back = [None, bank_slopes(1)]
@@ -354,10 +357,6 @@
     def query_part(s):
         return dot_tn(g_t[:, s * n : (s + 1) * n], cols[...])
 
-    qs_out[0] = query_part(3)
-    to_qs3 = send(qs_out.at[0], qs_in.at[0], 37, sibling)
-    qs_out[1] = query_part(1)
-    to_qs1 = send(qs_out.at[1], qs_in.at[1], 38, sibling)
 
     def z_back_copy(k, device):
         return remote(z_out.at[k], z_in.at[k], zb_send.at[k], zb_recv.at[k], device)
@@ -394,6 +393,10 @@
 
     to_pu = send(pu_out, pu_in, 36, partner)
 
+    qs_out[0] = query_part(3)
+    to_qs3 = send(qs_out.at[0], qs_in.at[0], 37, sibling)
+    qs_out[1] = query_part(1)
+    to_qs1 = send(qs_out.at[1], qs_in.at[1], 38, sibling)
     mine = query_part(2)
     to_qs3.wait_recv()
     qy_out[...] = (mine + qs_in[0]).astype(BF16)

time: 70.4 us -> 69.8 us (level)
  no operation moved by 1% of the time
where the time goes in v5:
time: 69.8 us; the launch traced here: 69.6 us
  Pallas kernels  69 us (99%)
    pallas_call x1, Pallas kernels, body(): pl.pallas_call(functools.partial(kernel, nz, nx), out_shape=results + (sm...  68 us

profile of v5, /device:TPU:1, one launch (start us, length us, event | category | flops | bytes accessed | tf_op | source)
XLA Modules:
  0.0 69.6 jit_solution(17586144778083416279)
XLA Ops:
  0.6 68.0 %shard_map.84 = (f32[1,128]{1,0:T(1,128)S(1)}, f32[128,1024]{1,0:T(8,128)S(1)}, f32[128,1024]{1,0:T(8,128)S(1)}, f32[4,8,128]{2,1,0:T(8,128)S(1)}, f32[4,8,128]{2,1,0:T(8,128)S(1)}, /*index=5*/f32[4,8,128]{2,1,0:T(8,128)S(1)}) custom-call(bf16[128,1024]{1,0:T(8,128)(2,1)} %q_in.1, bf16[128,1024]{1,0:T(8,128)(2,1)} %p_in.1, bf16[4,1024]{1,0:T(4,128)(2,1)} %bank_in.1, ...), custom_call_target="tpu_custom_call" | custom-call | tf_op jit(solution)/shard_map/pallas_call | solution.py:502
  68.6 1.0 %shard_map.85 = (f32[1,128]{1,0:T(1,128)}, f32[128,1024]{1,0:T(8,128)}, f32[128,1024]{1,0:T(8,128)}, f32[4,1024]{1,0:T(4,128)}) custom-call(f32[1,128]{1,0:T(1,128)S(1)} %get-tuple-element.14.loss, f32[128,1024]{1,0:T(8,128)S(1)} %get-tuple-element.15.qg, f32[128,1024]{1,0:T(8,128)S(1)} %get-tuple-element.16.pg, f32[4,8,128]{2,1,0:T(8,128)S(1)} %get-tuple-element.17.up_ref, ...), custom_call_target="tpu_custom_call" | custom-call | tf_op jit(solution)/shard_map/pallas_call | solution.py:546
